TPU v7x, 512 devices: a whole 4x4x16 slice. The times are simulated.
512 devices in a mesh: pole: 16 (over y, x_hi, core), grid: 32 (over z, x_lo).
Axes of the slice: x: 4 (x_hi: 2, x_lo: 2; x = x_hi * 2 + x_lo), y: 4, z: 16, core: 2. Of those that a mesh axis runs over, the one named last changes fastest.
Arguments:
- panel: bfloat16 [16, 2, 2048, 1024], P('pole', None, 'grid'), may hold values from -0.25 to 0.25
- inverse_blocks: bfloat16 [16, 32, 8, 2, 64, 64], P('pole', 'grid'), may hold values from -6 to 6
- diag_inverse: float32 [16, 1024, 2048], P('pole', 'grid'), may hold values from -6 to 6
- ancestors: int32 [32, 8], P('grid'), may hold values from 0 to 31, all different within a row
- pole_index: int32 [16], P('pole'), may hold values from 0 to 63
- weight_table: float32 [64, 2], replicated, may hold values from -1 to 1
Outputs:
- offdiag: bfloat16 [16, 2, 2048, 1024], P('pole', None, 'grid')
- density: float32 [1024, 1024], P('grid')
All inputs are finite; a program needn't handle non-finite values.
Results may differ from a plain program's by a relative error of at most 0.0007.
Values may be sent and summed in bfloat16 or wider, within the bound.
A program may use at most 64 MiB of HBM per device.

v0:
```python
import jax
import jax.numpy as jnp
from jax import lax
from jax.sharding import PartitionSpec as P


def shards(panel, inverse_blocks, diag_inverse, ancestors, pole_index, weight_table):
    count_grid = lax.axis_size("grid")
    rows_here = panel.shape[2]
    width = panel.shape[3]
    columns_ids = jnp.arange(count_grid, dtype=jnp.int32)
    onehot = (ancestors[0][:, None] == columns_ids[None, :]).astype(jnp.bfloat16)
    dense = jnp.einsum(
        "kn,kcab->canb", onehot, inverse_blocks[0, 0], preferred_element_type=jnp.float32
    )
    dense = dense.astype(jnp.bfloat16).reshape(2, rows_here, count_grid * rows_here)
    piece = lax.all_gather(panel, "grid", axis=2, tiled=True)
    span = piece.shape[2]
    left_real = dense[0]
    left_imag = dense[1]
    left = jnp.concatenate(
        [
            jnp.concatenate([left_real, -left_imag], axis=1),
            jnp.concatenate([left_imag, left_real], axis=1),
        ],
        axis=0,
    )
    right = piece[0].reshape(2 * span, width)
    product = jnp.dot(left, right, preferred_element_type=jnp.float32)
    off_full = (-product).reshape(2, rows_here, width)
    offdiag_local = off_full.astype(jnp.bfloat16).reshape(1, 2, rows_here, width)
    table_ids = jnp.arange(weight_table.shape[0], dtype=jnp.int32)
    selector = (table_ids == pole_index[0]).astype(jnp.float32)
    weights = jnp.sum(weight_table * selector[:, None], axis=0)
    stacked_panel = panel[0].reshape(2 * rows_here, width)
    off_real = off_full[0]
    off_imag = off_full[1]
    right_side = jnp.concatenate(
        [
            jnp.concatenate([off_real, off_imag], axis=1),
            jnp.concatenate([-off_imag, off_real], axis=1),
        ],
        axis=0,
    )
    picked = stacked_panel.astype(jnp.float32)
    both = lax.dot_general(
        picked,
        right_side,
        (((0,), (0,)), ((), ())),
        precision=lax.Precision.HIGHEST,
        preferred_element_type=jnp.float32,
    )
    summed = lax.psum_scatter(
        weights[0] * both[:, :width] - weights[1] * both[:, width:],
        "grid",
        scatter_dimension=0,
        tiled=True,
    )
    weighted = (
        weights[0] * diag_inverse[0][:, :width] - weights[1] * diag_inverse[0][:, width:] - summed
    )
    density = lax.psum(weighted, "pole")
    return (offdiag_local, density)


def solution(mesh):
    placed = (
        P("pole", None, "grid", None),
        P("pole", "grid", None, None, None, None),
        P("pole", "grid", None),
        P("grid", None),
        P("pole"),
        P(),
    )
    return jax.shard_map(
        shards,
        mesh=mesh,
        in_specs=placed,
        out_specs=(P("pole", None, "grid", None), P("grid", None)),
        check_vma=False,
    )
```

profile of v0, /device:TPU:1, one launch (start us, length us, event | category | flops | bytes accessed | tf_op | source)
XLA Modules:
  0.0 538.2 jit_solution(10676379237338288782)
XLA Ops:
  7.2 0.0 copy-start
  7.2 0.0 copy-start.3
  7.2 0.0 all-gather.2.cloned.1.call-start
  7.2 0.7 all-gather.2.cloned.1.call-update
  7.9 0.0 reduce-scatter.4.cloned.1.call-start
  8.0 0.1 copy-done
  8.1 1.2 fusion.1
  9.3 0.1 fusion.24
  9.4 0.5 squeeze.27
  9.9 0.5 squeeze.28
  11.0 0.0 copy-done.3
  11.1 0.1 multiply_reduce_fusion
  11.2 0.6 fusion.26
  11.8 198.2 %all-gather.2.cloned.1.call-done = bf16[1,2,2048,1024]{3,2,1,0:T(8,128)(2,1)} async-done(((bf16[1,2,64,1024]{3,2,1,0:T(8,128)(2,1)}), bf16[1,2,2048,1024]{3,2,1,0:T(8,128)(2,1)}) %all-gather.2.cloned.1.call-update) | async-done | bytes 8388624 | tf_op jit(solution)/shard_map/all_gather | solution.py:17
  210.0 0.0 copy-start.1
  210.0 5.5 %fusion.27 = (bf16[128,1024]{1,0:T(8,128)(2,1)}, f32[128,1024]{1,0:T(8,128)S(1)}) fusion(bf16[4096,1024]{1,0:T(8,128)(2,1)} %bitcast.30, bf16[64,2048]{1,0:T(8,128)(2,1)S(1)} %squeeze.27, bf16[64,2048]{1,0:T(8,128)(2,1)S(1)} %squeeze.28, bf16[64,2048]{1,0:T(8,128)(2,1)S(1)} %neg.9), kind=kOutput, calls=%fused_computation.37 | convolution fusion | flops 1078198272 | bytes 9961472 | tf_op jit(solution)/shard_map/dot_general | solution.py:29
  215.4 0.1 fusion.25
  215.5 0.0 copy-done.1
  215.5 3.5 convolution_bitcast_fusion
  219.0 4.2 fusion
  223.3 5.3 copy.15
  228.6 0.0 copy-start.2
  228.6 0.0 reduce-scatter.4.cloned.1.call-update
  228.6 0.0 all-reduce.2.cloned.1.call-start
  228.7 0.9 copy-done.2
  229.6 0.3 copy.12
  229.9 122.4 %reduce-scatter.4.cloned.1.call-done = f32[32,1024]{1,0:T(8,128)} async-done(((f32[1024,1024]{1,0:T(8,128)}), f32[32,1024]{1,0:T(8,128)}) %reduce-scatter.4.cloned.1.call-update) | async-done | bytes 131088
  352.3 1.1 copy.16
  353.4 2.2 fusion.17
  355.6 0.0 all-reduce.2.cloned.1.call-update
  355.6 174.2 %all-reduce.2.cloned.1.call-done = f32[32,1024]{0,1:T(8,128)} async-done(((f32[32,1024]{0,1:T(8,128)}), f32[32,1024]{0,1:T(8,128)}) %all-reduce.2.cloned.1.call-update) | async-done | bytes 131088 | tf_op jit(solution)/shard_map/psum | solution.py:62
  529.8 1.9 copy.13
  (2 shorter events, 0.0 us)
Async XLA Ops:
  7.2 1.0 copy-start
  7.2 3.9 copy-start.3
  7.2 202.8 %all-gather.2.cloned.1.call-start = ((), (), s32[]{:S(2)}) async-start(), calls=%async_computation.1 | async-start | bytes 8650752 | tf_op jit(solution)/shard_map/all_gather | solution.py:17
  7.9 344.4 %reduce-scatter.4.cloned.1.call-start = ((), (), s32[]{:S(2)}) async-start(), calls=%async_computation.3 | async-start | bytes 4325376
  210.0 5.6 %copy-start.1 = (bf16[1,2,64,1024]{3,2,1,0:T(8,128)(2,1)S(1)}, bf16[1,2,64,1024]{3,2,1,0:T(8,128)(2,1)}, u32[]{:S(2)}) copy-start(bf16[1,2,64,1024]{3,2,1,0:T(8,128)(2,1)} %param.6) | copy-start | bytes 786436
  228.6 0.9 copy-start.2
  228.6 301.1 %all-reduce.2.cloned.1.call-start = ((), (), s32[]{:S(2)}) async-start(), calls=%async_computation.2 | async-start | bytes 1048576 | tf_op jit(solution)/shard_map/psum | solution.py:62
Sparse Core Ops, SparseCore 0:
  10.1 199.8 all-gather.1
  228.8 123.4 reduce-scatter.3
  355.7 174.0 all-reduce.1
where the time goes:
time: 538 us
  waiting for transfers between devices  495 us (92%)
  between operations  14.5 us (3%)
  local copies, waits for them, and re-layouts  11.3 us (2%)
  matrix products  10.2 us (2%)
  other arithmetic  6.64 us (1%)
    all_gather x1, waiting for transfers between devices, shards(): piece = lax.all_gather(panel, 'grid', axis=2, tiled=True)  198 us
    psum x1, waiting for transfers between devices, shards(): density = lax.psum(weighted, 'pole')  174 us
    unnamed x4, waiting for transfers between devices  123 us
  transfers between devices with their start and end apart: 3, of which 3 were waited for; matrix products, arithmetic and copies ran while one was open for 1% of the time, Pallas kernels for 0%

commit v1 on v0

v1 whole, which is shorter than its diff:
```python
import functools

import jax
import jax.numpy as jnp
from jax import lax
from jax.experimental import pallas as pl
from jax.experimental.pallas import tpu as pltpu
from jax.sharding import PartitionSpec as P

MESH = pl.DeviceIdType.MESH
F32 = jnp.float32
BF16 = jnp.bfloat16
WAVES = 2
COLS = 512 // WAVES
LAG = (0, 1)
STEPS = 8


def kernel(
    anc_s, pole_s, table_s, panel, inv, diag, anc_v,
    off, dens,
    b00, b01, b10, b11, left_own, left_par, ancp_v, ancp_s, prow, pt, xs, xo,
    d0, d1, rc0, rc1, e0, e1, ry0, ry1, f0, f1, rz0, rz1, wd, dg, res,
    loc_sem, xc_send, xc_recv, misc_send, misc_recv, small_sem,
    ring_send, ring_recv, xo_send, xo_recv, c_send, c_recv, y_send, y_recv,
    z_send, z_recv, g_send, g_recv, n_send, n_recv,
):
    bufs = ((b00, b01), (b10, b11))
    ds, rcs, es, rys, fs, rzs = (d0, d1), (rc0, rc1), (e0, e1), (ry0, ry1), (f0, f1), (rz0, rz1)
    g = lax.axis_index("grid")
    p = lax.axis_index("pole")
    z, xl = g // 2, g % 2
    y, xh, core = p // 4, (p // 2) % 2, p % 2
    gx = 2 * z + 1 - xl
    gr = 2 * lax.rem(z + 1, 16) + xl
    gl = 2 * lax.rem(z + 15, 16) + xl
    pc = p + 1 - 2 * core
    xh_own = z // 8
    owner = xh == xh_own
    own = jnp.where(owner, 1, 0)
    own_self = jnp.where(jnp.logical_and(owner, core == xl), 1, 0)

    def at(pole, grid):
        return {"pole": pole, "grid": grid}

    def remote(src, dst, send, recv, pole, grid):
        return pltpu.make_async_remote_copy(
            src_ref=src, dst_ref=dst, send_sem=send, recv_sem=recv,
            device_id=at(pole, grid), device_id_type=MESH,
        )

    barrier = pltpu.get_barrier_semaphore()

    def hello(pole, grid):
        pl.semaphore_signal(barrier, inc=1, device_id=at(pole, grid), device_id_type=MESH)

    hello(p, gx)
    hello(p, gr)
    hello(p, gl)
    hello(pc, g)
    for k in range(1, 4):
        hello(lax.rem(y + k, 4) * 4 + xh * 2 + core, g)

    def not_me(pole, grid):
        return jnp.logical_or(pole != p, grid != g)

    def owner_of(n):
        return (n // 2) * 4 + xh_own * 2 + xl, 2 * z + n % 2

    def source(n):
        return y * 4 + (n // 16) * 2 + core, 2 * lax.rem(n, 16) + xl

    def to_final(n, carry):
        pole, grid = owner_of(n)

        @pl.when(not_me(pole, grid))
        def _():
            hello(pole, grid)

        return carry

    lax.fori_loop(0, 8, to_final, 0)

    @pl.when(owner)
    def _():
        def to_source(n, carry):
            pole, grid = source(n)

            @pl.when(not_me(pole, grid))
            def _():
                hello(pole, grid)

            return carry

        lax.fori_loop(0, 32, to_source, 0)

        def to_diag(n, carry):
            @pl.when(not_me(n, 2 * z + core))
            def _():
                hello(n, 2 * z + core)

            return carry

        lax.fori_loop(0, 16, to_diag, 0)

    index = pole_s[0]
    wr = table_s[index, 0]
    wi = table_s[index, 1]
    for k in range(0, 8, 2):
        left_own[:, 64 * k : 64 * k + 128] = jnp.concatenate(
            [inv[0, 0, k].reshape(128, 64), inv[0, 0, k + 1].reshape(128, 64)], axis=1
        )
    for h in range(2):
        wd[h] = wr * diag[0, :, 512 * h : 512 * h + 512] - wi * diag[0, :, 1024 + 512 * h : 1536 + 512 * h]

    def transpose_rows(rows, at_lane):
        for n in range(4):
            part = rows[:, :, 256 * n : 256 * n + 256].reshape(128, 256).astype(F32)
            pt[256 * n : 256 * n + 256, at_lane : at_lane + 128] = part.T.astype(BF16)

    transpose_rows(panel.at[0], 0)

    pl.semaphore_wait(barrier, 7 + 16 - own + 8 - own_self + 16 * own - own_self)

    pieces, locs = [], []
    for w in range(WAVES):
        for c in range(2):
            n = 2 * w + c
            piece = remote(
                panel.at[0, c, :, pl.ds((1 - xl) * 512 + w * COLS, COLS)], bufs[w][c].at[g],
                xc_send.at[n], xc_recv.at[n], p, gx,
            )
            piece.start()
            pieces.append(piece)
            loc = pltpu.make_async_copy(
                panel.at[0, c, :, pl.ds(xl * 512 + w * COLS, COLS)], bufs[w][c].at[g], loc_sem.at[n]
            )
            loc.start()
            locs.append(loc)
    misc = [
        remote(anc_v, ancp_v, misc_send.at[0], misc_recv.at[0], p, gx),
        remote(left_own, left_par, misc_send.at[1], misc_recv.at[1], p, gx),
        remote(panel.at[0], prow, misc_send.at[2], misc_recv.at[2], p, gx),
    ]

    def diag_copy(n):
        pole, grid = owner_of(n)
        rows = pl.ds(pl.multiple_of((n // 2) * 8, 8), 8)
        return pole, grid, remote(wd.at[n % 2, rows], dg.at[p], g_send.at[n], g_recv.at[p], pole, grid)

    def diag_start(n, carry):
        pole, grid, copy = diag_copy(n)

        @pl.when(not_me(pole, grid))
        def _():
            copy.start()

        return carry

    def ring(w, c, s, d):
        slot = lax.rem(z + (16 - s if d == 0 else s), 16)
        rows = pl.ds(2 * slot, 2) if s < STEPS - 1 else pl.ds(2 * slot + d, 1)
        ref = bufs[w][c].at[rows]
        return remote(ref, ref, ring_send.at[w, c, d, s], ring_recv.at[w, c, d, s], p, gr if d == 0 else gl)

    sends = []
    for t in range(max(LAG) + STEPS):
        for w in range(WAVES):
            s = t - LAG[w]
            if not 0 <= s < STEPS:
                continue
            for c in range(2):
                if s == 0:
                    locs[2 * w + c].wait()
                    pieces[2 * w + c].wait_recv()
                for d in range(2):
                    if s > 0:
                        ring(w, c, s - 1, d).wait_recv()
                    copy = ring(w, c, s, d)
                    copy.start()
                    sends.append(copy)
        if t == 1:
            for m in misc:
                m.start()
            lax.fori_loop(0, 8, diag_start, 0)
        if t == 4:
            for m in misc:
                m.wait_recv()
            small = pltpu.make_async_copy(ancp_v, ancp_s, small_sem)
            small.start()
            small.wait()
            transpose_rows(prow, 128)

    def product(w, which):
        left = (left_own, left_par)[which]
        ids = (anc_s, ancp_s)[which]
        rows = []
        for k in range(8):
            j = ids[0, k]
            rows.append(jnp.concatenate([bufs[w][0][j], bufs[w][1][j]], axis=1))
        right = jnp.concatenate(rows, axis=0)
        both = jnp.dot(left[...], right, preferred_element_type=F32)
        real = both[64:, COLS:] - both[:64, :COLS]
        imag = -(both[:64, COLS:] + both[64:, :COLS])
        return real, imag

    xsends, xlocs = [], []
    csends = []
    for w in range(WAVES):
        for c in range(2):
            for d in range(2):
                ring(w, c, STEPS - 1, d).wait_recv()
        terms = []
        for which in range(2):
            real, imag = product(w, which)
            dst = (xs, xo)[which]
            dst[w, 0] = real.astype(BF16)
            dst[w, 1] = imag.astype(BF16)
            terms.append(wr * real - wi * imag)
            terms.append(-wr * imag - wi * real)
        place = off.at[0, :, :, pl.ds(xl * 512 + w * COLS, COLS)]
        copy = remote(xo.at[w], place, xo_send.at[w], xo_recv.at[w], p, gx)
        copy.start()
        xsends.append(copy)
        copy = pltpu.make_async_copy(xs.at[w], place, loc_sem.at[w])
        copy.start()
        xlocs.append(copy)
        weighted = jnp.concatenate(terms, axis=0)
        high = weighted.astype(BF16)
        low = (weighted - high.astype(F32)).astype(BF16)
        split = jnp.concatenate([high, low], axis=1)
        for n in range(4):
            two = jnp.dot(pt[256 * n : 256 * n + 256, :], split, preferred_element_type=F32)
            ds[w][4 * n : 4 * n + 4] = (two[:, :COLS] + two[:, COLS:]).reshape(4, 64, COLS)
        copy = remote(
            ds[w].at[:, pl.ds(pl.multiple_of((1 - core) * 32, 32), 32)], rcs[w],
            c_send.at[w], c_recv.at[w], pc, g,
        )
        copy.start()
        csends.append(copy)

    ysends = []
    for w in range(WAVES):
        csends[w].wait_recv()
        es[w][...] = ds[w][:, pl.ds(pl.multiple_of(core * 32, 32), 32)] + rcs[w][...]
        for k in range(1, 4):
            to = lax.rem(y + k, 4)
            copy = remote(
                es[w].at[:, pl.ds(pl.multiple_of(to * 8, 8), 8)], rys[w].at[k - 1],
                y_send.at[w, k - 1], y_recv.at[w, k - 1], to * 4 + xh * 2 + core, g,
            )
            copy.start()
            ysends.append(copy)

    def z_copy(w, to):
        pole, grid = y * 4 + (to // 8) * 2 + core, 2 * to + xl
        me = xh * 16 + z
        return pole, grid, remote(
            fs[w].at[to], rzs[w].at[me], z_send.at[w, to], z_recv.at[w, me], pole, grid
        )

    def z_start(w, to, carry):
        pole, grid, copy = z_copy(w, to)

        @pl.when(not_me(pole, grid))
        def _():
            copy.start()

        return carry

    for w in range(WAVES):
        for k in range(3):
            ysends[3 * w + k].wait_recv()
        fs[w][...] = es[w][:, pl.ds(pl.multiple_of(y * 8, 8), 8)] + rys[w][0] + rys[w][1] + rys[w][2]
        lax.fori_loop(0, 16, functools.partial(z_start, w), 0)

    @pl.when(owner)
    def _():
        def diag_wait(n, total):
            @pl.when(not_me(n, 2 * z + core))
            def _():
                remote(wd.at[0, pl.ds(0, 8)], dg.at[n], g_send.at[0], g_recv.at[n], n, 2 * z + core).wait_recv()

            return total

        lax.fori_loop(0, 16, diag_wait, 0)

        @pl.when(core == xl)
        def _():
            dg[p] = wd[xl, pl.ds(pl.multiple_of(y * 8, 8), 8)]

        total = dg[0]
        for n in range(1, 16):
            total = total + dg[n]

        for w in range(WAVES):
            def z_wait(n, carry):
                pole, grid = source(n)

                @pl.when(not_me(pole, grid))
                def _():
                    remote(fs[w].at[0], rzs[w].at[n], z_send.at[w, 0], z_recv.at[w, n], pole, grid).wait_recv()

                return carry

            lax.fori_loop(0, 32, z_wait, 0)
            rzs[w][xh * 16 + z] = fs[w][z]
            part = rzs[w][0]
            for n in range(1, 32):
                part = part + rzs[w][n]
            res[:, w * COLS : w * COLS + COLS] = total[:, w * COLS : w * COLS + COLS] - part

    me = y * 2 + xl

    def final_copy(n):
        place = dens.at[pl.ds(pl.multiple_of(y * 8, 8), 8), pl.ds(pl.multiple_of(xl * 512, 512), 512)]
        return remote(res, place, n_send.at[n], n_recv.at[me], n, 2 * z + core)

    @pl.when(owner)
    def _():
        def final_start(n, carry):
            @pl.when(not_me(n, 2 * z + core))
            def _():
                final_copy(n).start()

            return carry

        lax.fori_loop(0, 16, final_start, 0)

        @pl.when(core == xl)
        def _():
            place = dens.at[pl.ds(pl.multiple_of(y * 8, 8), 8), pl.ds(pl.multiple_of(xl * 512, 512), 512)]
            copy = pltpu.make_async_copy(res, place, small_sem)
            copy.start()
            copy.wait()

    def final_wait(n, carry):
        pole, grid = owner_of(n)

        @pl.when(not_me(pole, grid))
        def _():
            place = dens.at[pl.ds(pl.multiple_of((n // 2) * 8, 8), 8), pl.ds(pl.multiple_of(lax.rem(n, 2) * 512, 512), 512)]
            remote(res, place, n_send.at[0], n_recv.at[n], pole, grid).wait_recv()

        return carry

    lax.fori_loop(0, 8, final_wait, 0)

    for copy in xsends:
        copy.wait_recv()
    for copy in xlocs:
        copy.wait()
    for copy in sends + pieces + misc + xsends + csends + ysends:
        copy.wait_send()

    def diag_done(n, carry):
        pole, grid, copy = diag_copy(n)

        @pl.when(not_me(pole, grid))
        def _():
            copy.wait_send()

        return carry

    lax.fori_loop(0, 8, diag_done, 0)
    for w in range(WAVES):
        def z_done(to, carry):
            pole, grid, copy = z_copy(w, to)

            @pl.when(not_me(pole, grid))
            def _():
                copy.wait_send()

            return carry

        lax.fori_loop(0, 16, z_done, 0)

    @pl.when(owner)
    def _():
        def final_done(n, carry):
            @pl.when(not_me(n, 2 * z + core))
            def _():
                final_copy(n).wait_send()

            return carry

        lax.fori_loop(0, 16, final_done, 0)


def shards(panel, inverse_blocks, diag_inverse, ancestors, pole_index, weight_table):
    vmem = pl.BlockSpec(memory_space=pltpu.VMEM)
    smem = pl.BlockSpec(memory_space=pltpu.SMEM)
    dma = pltpu.SemaphoreType.DMA
    per_wave = lambda shape, kind: [pltpu.VMEM(shape, kind)] * WAVES
    scratch = [pltpu.VMEM((32, 64, COLS), BF16)] * (2 * WAVES)
    scratch += [
        pltpu.VMEM((128, 512), BF16),
        pltpu.VMEM((128, 512), BF16),
        pltpu.VMEM((1, 8), jnp.int32),
        pltpu.SMEM((1, 8), jnp.int32),
        pltpu.VMEM((2, 64, 1024), BF16),
        pltpu.VMEM((1024, 256), BF16),
        pltpu.VMEM((WAVES, 2, 64, COLS), BF16),
        pltpu.VMEM((WAVES, 2, 64, COLS), BF16),
    ]
    scratch += per_wave((16, 64, COLS), F32)
    scratch += per_wave((16, 32, COLS), F32)
    scratch += per_wave((16, 32, COLS), F32)
    scratch += per_wave((3, 16, 8, COLS), F32)
    scratch += per_wave((16, 8, COLS), F32)
    scratch += per_wave((32, 8, COLS), F32)
    scratch += [
        pltpu.VMEM((2, 32, 512), F32),
        pltpu.VMEM((16, 8, 512), F32),
        pltpu.VMEM((8, 512), F32),
    ]
    scratch += [
        dma((4,)), dma((4,)), dma((4,)), dma((3,)), dma((3,)), dma,
        dma((WAVES, 2, 2, STEPS)), dma((WAVES, 2, 2, STEPS)),
        dma((WAVES,)), dma((WAVES,)), dma((WAVES,)), dma((WAVES,)),
        dma((WAVES, 3)), dma((WAVES, 3)), dma((WAVES, 16)), dma((WAVES, 32)),
        dma((8,)), dma((16,)), dma((16,)), dma((8,)),
    ]
    return pl.pallas_call(
        kernel,
        out_shape=(
            jax.ShapeDtypeStruct(panel.shape, BF16),
            jax.ShapeDtypeStruct((32, 1024), F32),
        ),
        in_specs=[smem, smem, smem, vmem, vmem, vmem, vmem],
        out_specs=(vmem, vmem),
        scratch_shapes=scratch,
        compiler_params=pltpu.CompilerParams(
            collective_id=1, has_side_effects=True, vmem_limit_bytes=40 << 20
        ),
    )(ancestors, pole_index, weight_table, panel, inverse_blocks, diag_inverse, ancestors)


def solution(mesh):
    placed = (
        P("pole", None, "grid", None),
        P("pole", "grid", None, None, None, None),
        P("pole", "grid", None),
        P("grid", None),
        P("pole"),
        P(),
    )
    return jax.shard_map(
        shards,
        mesh=mesh,
        in_specs=placed,
        out_specs=(P("pole", None, "grid", None), P("grid", None)),
        check_vma=False,
    )
```

time: 538 us -> 107 us (0.20)
  waiting for transfers between devices: 495 us -> 0 us
  Pallas kernels: 0 us -> 100 us
  between operations: 14.5 us -> 1.32 us
  matrix products: 10.2 us -> 0 us
  other arithmetic: 6.64 us -> 0 us
  local copies, waits for them, and re-layouts: 11.3 us -> 4.87 us
    all_gather x1 -> x0, waiting for transfers between devices: 198 us -> none  [shards(): piece = lax.all_gather(panel, 'grid', axis=2, tiled=True)]
    psum x1 -> x0, waiting for transfers between devices: 174 us -> none  [shards(): density = lax.psum(weighted, 'pole')]
    unnamed x4 -> x0, waiting for transfers between devices: 123 us -> none
    pallas_call x0 -> x1, Pallas kernels: none -> 100 us  [shards(): pl.pallas_call(kernel, out_shape=(jax.ShapeDtypeStruct(panel.shape, BF16)...]
    dot_general x3 -> x0, matrix products: 10.2 us -> none  [the longest x1 5.47 us: shards(): product = jnp.dot(left, right, preferred_element_type=jnp.float32)]
    sub x2 -> x0, other arithmetic: 6.4 us -> none  [the longest x1 4.25 us: shards(): weights[0] * both[:, :width] - weights[1] * both[:, width:]]
  transfers between devices with their start and end apart: 3 -> 0, of which waited for: 3 -> 0; matrix products, arithmetic and copies ran while one was open for 1% -> 0% of each run, Pallas kernels for 0% -> 0%
where the time goes in v1:
time: 107 us; the launch traced here: 106 us
  Pallas kernels  100 us (93%)
  local copies, waits for them, and re-layouts  4.87 us (5%)
  between operations  1.32 us (1%)
    pallas_call x1, Pallas kernels, shards(): pl.pallas_call(kernel, out_shape=(jax.ShapeDtypeStruct(panel.shape, BF16)...  100 us
    unnamed x13, local copies, waits for them, and re-layouts  4.87 us

profile of v1, /device:TPU:1, one launch (start us, length us, event | category | flops | bytes accessed | tf_op | source)
XLA Modules:
  0.0 106.3 jit_solution(497990407183704854)
XLA Ops:
  0.6 0.0 copy-start.4
  1.3 0.0 copy-done.4
  1.3 0.0 copy-start.3
  1.3 0.1 copy.8.table_s
  1.4 0.6 copy-done.3
  2.0 0.0 copy-start
  2.0 0.9 copy-done
  2.9 0.0 copy-start.1
  2.9 0.9 copy-done.1
  3.9 0.0 copy-start.2
  3.9 0.9 copy-done.2
  4.8 100.1 %shard_map.77 = (bf16[1,2,64,1024]{3,2,1,0:T(8,128)(2,1)S(1)}, f32[32,1024]{1,0:T(8,128)S(1)}) custom-call(s32[1,8]{1,0:T(1,128)S(1)} %copy-done.3, s32[1]{0:T(128)S(6)} %copy.11.pole_s, f32[64,2]{1,0:T(8,128)S(1)} %copy.8.table_s, bf16[1,2,64,1024]{3,2,1,0:T(8,128)(2,1)S(1)} %copy-done, bf16[1,1,8,2,64,64]{5,4,3,2,1,0:T(8,128)(2,1)S(1)} %copy-done.1, ...), custom_call_target="tpu_custom_call" | custom-call | tf_op jit(solution)/shard_map/pallas_call | solution.py:424
  104.9 0.7 copy.12
  105.6 0.7 copy.13
Async XLA Ops:
  0.6 0.7 copy-start.4
  1.3 0.7 copy-start.3
  2.0 0.9 copy-start
  2.9 0.9 copy-start.1
  3.9 0.9 copy-start.2

commit v2 on v0

v2 whole, which is shorter than its diff:
```python
import jax
import jax.numpy as jnp
from jax import lax
from jax.experimental import pallas as pl
from jax.experimental.pallas import tpu as pltpu
from jax.sharding import PartitionSpec as P

MESH = pl.DeviceIdType.MESH
F32 = jnp.float32
BF16 = jnp.bfloat16
NEAR = (0, 1, 7, 2, 6, 3, 5, 4)


def kernel(
    anc_v, pole_s, table_s, panel_h, inv_h, diag_h,
    off, dens,
    panel, inv, diag, left, wt, pr, lr, buf, lbuf, ancb_v, ancb_s, wtb, prow, xb, yt, d, rx, fb, rz, wd, dg, res,
    in_sem, one_sem,
    p_send, p_recv, l_send, l_recv, pz_send, pz_recv, lz_send, lz_recv, a_send, a_recv, w_send, w_recv,
    xg_send, xg_recv, yg_send, yg_recv, cg_send, cg_recv, cr_send, cr_recv,
    ly_send, ly_recv, lc_send, lc_recv,
    g_send, g_recv, r_send, o_recv, xr_send, xr_recv, z_send, z_recv, n_send, n_recv,
):
    g = lax.axis_index("grid")
    p = lax.axis_index("pole")
    z, xl = g // 2, g % 2
    y, xh, core = p // 4, (p // 2) % 2, p % 2
    u = 2 * y + core
    x = 2 * xh + xl
    half = z // 2
    odd = z % 2
    relay = odd == xh

    def remote(src, dst, send, recv, pole, grid):
        return pltpu.make_async_remote_copy(
            src_ref=src, dst_ref=dst, send_sem=send, recv_sem=recv,
            device_id={"pole": pole, "grid": grid}, device_id_type=MESH,
        )

    def other(pole, grid):
        return jnp.logical_or(pole != p, grid != g)

    def each(count, body):
        def step(n, carry):
            body(n)
            return carry

        lax.fori_loop(0, count, step, 0)

    barrier = pltpu.get_barrier_semaphore()

    def hello(pole, grid):
        @pl.when(other(pole, grid))
        def _():
            pl.semaphore_signal(barrier, inc=1, device_id={"pole": pole, "grid": grid}, device_id_type=MESH)

    each(16, lambda n: hello(p, 2 * n + xl))
    each(32, lambda n: hello(n // 2, 2 * z + n % 2))
    loads = [
        pltpu.make_async_copy(panel_h, panel, in_sem.at[0]),
        pltpu.make_async_copy(inv_h, inv, in_sem.at[1]),
        pltpu.make_async_copy(diag_h, diag, in_sem.at[2]),
    ]
    for load in loads:
        load.start()
    pl.semaphore_wait(barrier, 15 + 31)

    def target(n):
        return (n // 2) * 4 + odd * 2 + n % 2

    def aligned(n, size):
        return pl.ds(pl.multiple_of(n * size, size), size)

    def send_p(n):
        return remote(panel.at[0, :, :, aligned(n, 128)], pr.at[p], p_send.at[n], p_recv.at[p], target(n), g)

    def left_part(n):
        return left.at[aligned(n % 2, 64), aligned(n // 2, 128)]

    def send_l(n):
        return remote(left_part(n), lr.at[p], l_send.at[n], l_recv.at[p], target(n), g)

    def start_first(make):
        def start(n):
            @pl.when(target(n) != p)
            def _():
                make(n).start()

        each(8, start)

    loads[0].wait()
    start_first(send_p)
    own_p = pltpu.make_async_copy(panel.at[0, :, :, aligned(u, 128)], pr.at[p], one_sem.at[0])
    own_p.start()

    loads[1].wait()
    for k in range(0, 8, 2):
        left[:, 64 * k : 64 * k + 128] = jnp.concatenate(
            [inv[0, 0, k].reshape(128, 64), inv[0, 0, k + 1].reshape(128, 64)], axis=1
        )
    start_first(send_l)
    own_l = pltpu.make_async_copy(left_part(u), lr.at[p], one_sem.at[1])
    own_l.start()
    own_p.wait()
    own_l.wait()

    index = pole_s[0]
    my_wr = table_s[index, 0]
    my_wi = table_s[index, 1]
    is_real = lax.broadcasted_iota(jnp.int32, (8, 128), 0) == 0
    wt[...] = jnp.where(is_real, my_wr, my_wi)

    def send_a(q):
        return remote(anc_v, ancb_v.at[half], a_send.at[q], a_recv.at[half], p, 2 * q + xl)

    def send_w(q):
        return remote(wt, wtb, w_send.at[q], w_recv, q, g)

    def start_a(q):
        @pl.when(q != z)
        def _():
            send_a(q).start()

    def start_w(q):
        @pl.when(q != p)
        def _():
            send_w(q).start()

    row = 4 * half + 2 * odd + xl
    l_place = (aligned(core, 64), aligned(y, 128))

    def send_pz(q):
        return remote(pr.at[q], buf.at[row], pz_send.at[q], pz_recv.at[half], p, 2 * q + xl)

    def send_lz(q):
        return remote(lr.at[q], lbuf.at[(half,) + l_place], lz_send.at[q], lz_recv.at[half], p, 2 * q + xl)

    @pl.when(relay)
    def _():
        for far in (8, 7, 9, 6, 10, 5, 11, 4, 12, 3, 13, 2, 14, 1, 15):
            q = lax.rem(z + far, 16)

            @pl.when(q != p)
            def _():
                remote(pr.at[0], pr.at[q], p_send.at[0], p_recv.at[q], q, g).wait_recv()

            send_pz(q).start()

        for far in (8, 7, 9, 6, 10, 5, 11, 4, 12, 3, 13, 2, 14, 1, 15):
            q = lax.rem(z + far, 16)

            @pl.when(q != p)
            def _():
                remote(lr.at[0], lr.at[q], l_send.at[0], l_recv.at[q], q, g).wait_recv()

            send_lz(q).start()

        @pl.when(z != p)
        def _():
            remote(pr.at[0], pr.at[z], p_send.at[0], p_recv.at[z], z, g).wait_recv()
            remote(lr.at[0], lr.at[z], l_send.at[0], l_recv.at[z], z, g).wait_recv()

        buf[row] = pr[z]
        copies = [
            pltpu.make_async_copy(lr.at[z], lbuf.at[(half,) + l_place], one_sem.at[0]),
            pltpu.make_async_copy(anc_v, ancb_v.at[half], one_sem.at[1]),
        ]
        for copy in copies:
            copy.start()
        each(16, start_a)
        for copy in copies:
            copy.wait()

    @pl.when(z == p)
    def _():
        wtb[...] = wt[...]
        each(16, start_w)

    loads[2].wait()
    for n in range(8):
        wd[n] = my_wr * diag[0, :, 128 * n : 128 * n + 128] - my_wi * diag[0, :, 1024 + 128 * n : 1152 + 128 * n]

    def holder(n):
        return (n // 4) * 4 + xl * 2 + (n // 2) % 2, 2 * z + n % 2

    def send_d(n):
        pole, grid = holder(n)
        return remote(wd.at[n // 2, aligned(n % 2, 16)], dg.at[p], g_send.at[n], g_recv.at[p], pole, grid)

    def start_d(n):
        pole, grid = holder(n)

        @pl.when(other(pole, grid))
        def _():
            send_d(n).start()

    each(16, start_d)

    @pl.when(xl == xh)
    def _():
        dg[p] = wd[u, aligned(xl, 16)]

    def at_x(k):
        to = lax.rem(x + k, 4)
        return y * 4 + (to // 2) * 2 + core, 2 * z + to % 2

    def at_y(k):
        return lax.rem(y + k, 4) * 4 + xh * 2 + core

    partner = p + 1 - 2 * core

    def source(m):
        return p, 2 * (2 * m + xh) + xl

    def wait_other(m, make):
        @pl.when(2 * m + xh != z)
        def _():
            make().wait_recv()

    def send_x(k, m):
        block = buf.at[4 * m + x]
        pole, grid = at_x(k)
        return remote(block, block, xg_send.at[k - 1, m], xg_recv.at[k - 1, m], pole, grid)

    def send_y(k, m):
        return remote(
            buf.at[4 * m + x], prow.at[u, m], yg_send.at[k - 1, m], yg_recv.at[k - 1, m], at_y(k), g
        )

    def send_c(m):
        return remote(buf.at[4 * m + x], prow.at[u, m], cg_send.at[m], cg_recv.at[m], partner, g)

    for near in NEAR:
        m = lax.rem(half + near, 8)
        wait_other(m, lambda: remote(pr.at[0], buf.at[4 * m + x], pz_send.at[0], pz_recv.at[m], *source(m)))
        for k in (2, 1, 3):
            send_y(k, m).start()
            send_x(k, m).start()
        send_c(m).start()
        prow[u, m] = buf[4 * m + x]

    own_part = (slice(None), aligned(core, 64), aligned(y, 128))

    def send_ly(k):
        part = lbuf.at[own_part]
        return remote(part, part, ly_send.at[k - 1], ly_recv.at[k - 1], at_y(k), g)

    for near in NEAR:
        m = lax.rem(half + near, 8)
        wait_other(m, lambda: remote(lr.at[0], lbuf.at[(m,) + l_place], lz_send.at[0], lz_recv.at[m], *source(m)))
        wait_other(m, lambda: remote(anc_v, ancb_v.at[m], a_send.at[0], a_recv.at[m], *source(m)))

    @pl.when(z != p)
    def _():
        remote(wt, wtb, w_send.at[0], w_recv, z, g).wait_recv()

    for k in (2, 1, 3):
        send_ly(k).start()
    small = pltpu.make_async_copy(ancb_v, ancb_s, one_sem.at[0])
    small.start()
    small.wait()

    def send_cr(k):
        came = prow.at[2 * lax.rem(y + 4 - k, 4) + core]
        return remote(came, came, cr_send.at[k - 1], cr_recv.at[k - 1], partner, g)

    for k in (1, 3, 2):
        def wait_y(m):
            send_y(k, m).wait_recv()

        each(8, wait_y)
        send_cr(k).start()
    for k in range(1, 4):
        send_ly(k).wait_recv()
    rows_here = lbuf.at[:, aligned(core, 64), :]
    send_lc = remote(rows_here, rows_here, lc_send, lc_recv, partner, g)
    send_lc.start()
    for k in range(1, 4):
        each(8, lambda m: send_x(k, m).wait_recv())
    send_lc.wait_recv()

    wr = wtb[0:1, :]
    wi = wtb[1:2, :]

    off_place = off.at[0, :, :, aligned(u, 128)]

    def send_r(m):
        return remote(xb.at[m], off_place, r_send.at[m], o_recv.at[u], z, 2 * (2 * m + xh) + xl)

    def start_r(m):
        @pl.when(other(z, 2 * (2 * m + xh) + xl))
        def _():
            send_r(m).start()

    for m in range(8):
        rows = []
        for k in range(8):
            j = ancb_s[m, 0, k]
            rows.append(jnp.concatenate([buf[j, 0], buf[j, 1]], axis=1))
        both = jnp.dot(lbuf[m], jnp.concatenate(rows, axis=0), preferred_element_type=F32)
        real = both[64:, 128:] - both[:64, :128]
        imag = -(both[:64, 128:] + both[64:, :128])
        xb[m, 0] = real.astype(BF16)
        xb[m, 1] = imag.astype(BF16)
        start_r(m)
        term = jnp.concatenate([wr * real - wi * imag, -wr * imag - wi * real], axis=0).T
        high = term.astype(BF16)
        yt[0:128, 128 * m : 128 * m + 128] = high
        yt[128:256, 128 * m : 128 * m + 128] = (term - high.astype(F32)).astype(BF16)

    each(8, lambda m: send_c(m).wait_recv())
    for k in range(1, 4):
        send_cr(k).wait_recv()
    for n in range(4):
        columns = jnp.concatenate([prow[2 * n].reshape(1024, 128), prow[2 * n + 1].reshape(1024, 128)], axis=1)
        two = jnp.dot(yt[...], columns, preferred_element_type=F32)
        one = two[:128] + two[128:]
        d[4 * n : 4 * n + 2] = one[:, :128].T.reshape(2, 64, 128)
        d[4 * n + 2 : 4 * n + 4] = one[:, 128:].T.reshape(2, 64, 128)

    def send_xr(k):
        pole, grid = at_x(k)
        return remote(d.at[:, aligned(lax.rem(x + k, 4), 16)], rx.at[k - 1], xr_send.at[k - 1], xr_recv.at[k - 1], pole, grid)

    for k in (2, 1, 3):
        send_xr(k).start()
    for k in range(1, 4):
        send_xr(k).wait_recv()
    fb[...] = d[:, aligned(x, 16)] + rx[0] + rx[1] + rx[2]

    def send_z(k):
        to = lax.rem(z + k, 16)
        return remote(fb.at[to], rz.at[z], z_send.at[k], z_recv.at[z], p, 2 * to + xl)

    each(15, lambda n: send_z(n + 1).start())

    @pl.when(jnp.logical_and(z == p, relay))
    def _():
        home = pltpu.make_async_copy(xb.at[half], off_place, one_sem.at[1])
        home.start()
        home.wait()

    def wait_d(n):
        @pl.when(other(n, 2 * z + xh))
        def _():
            remote(wd.at[0, pl.ds(0, 16)], dg.at[n], g_send.at[0], g_recv.at[n], n, 2 * z + xh).wait_recv()

    each(16, wait_d)
    total = dg[0]
    for n in range(1, 16):
        total = total + dg[n]

    def wait_z(n):
        @pl.when(n != z)
        def _():
            remote(fb.at[0], rz.at[n], z_send.at[0], z_recv.at[n], p, 2 * n + xl).wait_recv()

    each(16, wait_z)
    rz[z] = fb[z]
    part = rz[0]
    for n in range(1, 16):
        part = part + rz[n]
    res[...] = total - part

    place = dens.at[aligned(xl, 16), aligned(u, 128)]
    me = 2 * u + xl

    def send_n(n):
        return remote(res, place, n_send.at[n], n_recv.at[me], n, 2 * z + xh)

    def start_n(n):
        @pl.when(other(n, 2 * z + xh))
        def _():
            send_n(n).start()

    each(16, start_n)

    @pl.when(xl == xh)
    def _():
        copy = pltpu.make_async_copy(res, place, one_sem.at[2])
        copy.start()
        copy.wait()

    def wait_n(n):
        pole, grid = holder(n)

        @pl.when(other(pole, grid))
        def _():
            there = dens.at[aligned(n % 2, 16), aligned(n // 2, 128)]
            remote(res, there, n_send.at[0], n_recv.at[n], pole, grid).wait_recv()

    each(16, wait_n)

    def wait_o(n):
        @pl.when(other(target(n), 2 * p + xl))
        def _():
            remote(xb.at[0], off.at[0, :, :, aligned(n, 128)], r_send.at[0], o_recv.at[n], target(n), 2 * p + xl).wait_recv()

    each(8, wait_o)

    def done_first(n):
        @pl.when(target(n) != p)
        def _():
            send_p(n).wait_send()
            send_l(n).wait_send()

    each(8, done_first)

    @pl.when(relay)
    def _():
        def done_z(q):
            @pl.when(q != z)
            def _():
                send_pz(q).wait_send()
                send_lz(q).wait_send()
                send_a(q).wait_send()

        each(16, done_z)

    @pl.when(z == p)
    def _():
        def done_w(q):
            @pl.when(q != p)
            def _():
                send_w(q).wait_send()

        each(16, done_w)

    def done_d(n):
        pole, grid = holder(n)

        @pl.when(other(pole, grid))
        def _():
            send_d(n).wait_send()

    each(16, done_d)

    def done_m(m):
        for k in range(1, 4):
            send_y(k, m).wait_send()
            send_x(k, m).wait_send()
        send_c(m).wait_send()

        @pl.when(other(z, 2 * (2 * m + xh) + xl))
        def _():
            send_r(m).wait_send()

    each(8, done_m)
    for k in range(1, 4):
        send_ly(k).wait_send()
        send_cr(k).wait_send()
        send_xr(k).wait_send()
    send_lc.wait_send()
    each(15, lambda n: send_z(n + 1).wait_send())

    def done_n(n):
        @pl.when(other(n, 2 * z + xh))
        def _():
            send_n(n).wait_send()

    each(16, done_n)


def shards(panel, inverse_blocks, diag_inverse, ancestors, pole_index, weight_table):
    vmem = pl.BlockSpec(memory_space=pltpu.VMEM)
    smem = pl.BlockSpec(memory_space=pltpu.SMEM)
    hbm = pl.BlockSpec(memory_space=pltpu.HBM)
    dma = pltpu.SemaphoreType.DMA
    scratch = [
        pltpu.VMEM((1, 2, 64, 1024), BF16),
        pltpu.VMEM((1, 1, 8, 2, 64, 64), BF16),
        pltpu.VMEM((1, 32, 2048), F32),
        pltpu.VMEM((128, 512), BF16),
        pltpu.VMEM((8, 128), F32),
        pltpu.VMEM((16, 2, 64, 128), BF16),
        pltpu.VMEM((16, 64, 128), BF16),
        pltpu.VMEM((32, 2, 64, 128), BF16),
        pltpu.VMEM((8, 128, 512), BF16),
        pltpu.VMEM((8, 1, 8), jnp.int32),
        pltpu.SMEM((8, 1, 8), jnp.int32),
        pltpu.VMEM((8, 128), F32),
        pltpu.VMEM((8, 8, 2, 64, 128), BF16),
        pltpu.VMEM((8, 2, 64, 128), BF16),
        pltpu.VMEM((256, 1024), BF16),
        pltpu.VMEM((16, 64, 128), F32),
        pltpu.VMEM((3, 16, 16, 128), F32),
        pltpu.VMEM((16, 16, 128), F32),
        pltpu.VMEM((16, 16, 128), F32),
        pltpu.VMEM((8, 32, 128), F32),
        pltpu.VMEM((16, 16, 128), F32),
        pltpu.VMEM((16, 128), F32),
        dma((3,)), dma((4,)),
        dma((8,)), dma((16,)), dma((8,)), dma((16,)),
        dma((16,)), dma((8,)), dma((16,)), dma((8,)), dma((16,)), dma((8,)), dma((16,)), dma,
        dma((3, 8)), dma((3, 8)), dma((3, 8)), dma((3, 8)), dma((8,)), dma((8,)), dma((3,)), dma((3,)),
        dma((3,)), dma((3,)), dma, dma,
        dma((16,)), dma((16,)), dma((8,)), dma((8,)), dma((3,)), dma((3,)),
        dma((16,)), dma((16,)), dma((16,)), dma((16,)),
    ]
    return pl.pallas_call(
        kernel,
        out_shape=(
            jax.ShapeDtypeStruct(panel.shape, BF16),
            jax.ShapeDtypeStruct((32, 1024), F32),
        ),
        in_specs=[vmem, smem, smem, hbm, hbm, hbm],
        out_specs=(vmem, vmem),
        scratch_shapes=scratch,
        compiler_params=pltpu.CompilerParams(
            collective_id=1, has_side_effects=True, vmem_limit_bytes=32 << 20
        ),
    )(ancestors, pole_index, weight_table, panel, inverse_blocks, diag_inverse)


def solution(mesh):
    placed = (
        P("pole", None, "grid", None),
        P("pole", "grid", None, None, None, None),
        P("pole", "grid", None),
        P("grid", None),
        P("pole"),
        P(),
    )
    return jax.shard_map(
        shards,
        mesh=mesh,
        in_specs=placed,
        out_specs=(P("pole", None, "grid", None), P("grid", None)),
        check_vma=False,
    )
```

time: 538 us -> 105 us (0.20)
  waiting for transfers between devices: 495 us -> 0 us
  Pallas kernels: 0 us -> 98.9 us
  between operations: 14.5 us -> 1.32 us
  matrix products: 10.2 us -> 0 us
  other arithmetic: 6.64 us -> 0 us
  local copies, waits for them, and re-layouts: 11.3 us -> 4.87 us
    all_gather x1 -> x0, waiting for transfers between devices: 198 us -> none  [shards(): piece = lax.all_gather(panel, 'grid', axis=2, tiled=True)]
    psum x1 -> x0, waiting for transfers between devices: 174 us -> none  [shards(): density = lax.psum(weighted, 'pole')]
    unnamed x4 -> x0, waiting for transfers between devices: 123 us -> none
    pallas_call x0 -> x1, Pallas kernels: none -> 98.9 us  [shards(): pl.pallas_call(kernel, out_shape=(jax.ShapeDtypeStruct(panel.shape, BF16)...]
    dot_general x3 -> x0, matrix products: 10.2 us -> none  [the longest x1 5.47 us: shards(): product = jnp.dot(left, right, preferred_element_type=jnp.float32)]
    sub x2 -> x0, other arithmetic: 6.4 us -> none  [the longest x1 4.25 us: shards(): weights[0] * both[:, :width] - weights[1] * both[:, width:]]
  transfers between devices with their start and end apart: 3 -> 0, of which waited for: 3 -> 0; matrix products, arithmetic and copies ran while one was open for 1% -> 0% of each run, Pallas kernels for 0% -> 0%
where the time goes in v2:
time: 105 us
  Pallas kernels  98.9 us (94%)
  local copies, waits for them, and re-layouts  4.87 us (5%)
  between operations  1.32 us (1%)
    pallas_call x1, Pallas kernels, shards(): pl.pallas_call(kernel, out_shape=(jax.ShapeDtypeStruct(panel.shape, BF16)...  98.9 us
    unnamed x13, local copies, waits for them, and re-layouts  4.87 us

profile of v2, /device:TPU:1, one launch (start us, length us, event | category | flops | bytes accessed | tf_op | source)
XLA Modules:
  0.0 105.0 jit_solution(14950568184926311355)
XLA Ops:
  0.6 0.0 copy-start.4
  1.3 0.0 copy-done.4
  1.3 0.0 copy-start.3
  1.3 0.1 copy.8.table_s
  1.4 0.6 copy-done.3
  2.0 0.0 copy-start
  2.0 0.9 copy-done
  2.9 0.0 copy-start.1
  2.9 0.9 copy-done.1
  3.9 0.0 copy-start.2
  3.9 0.9 copy-done.2
  4.8 98.9 %shard_map.77 = (bf16[1,2,64,1024]{3,2,1,0:T(8,128)(2,1)S(1)}, f32[32,1024]{1,0:T(8,128)S(1)}) custom-call(s32[1,8]{1,0:T(1,128)S(1)} %copy-done.3, s32[1]{0:T(128)S(6)} %copy.11.pole_s, f32[64,2]{1,0:T(8,128)S(1)} %copy.8.table_s, bf16[1,2,64,1024]{3,2,1,0:T(8,128)(2,1)S(1)} %copy-done, bf16[1,1,8,2,64,64]{5,4,3,2,1,0:T(8,128)(2,1)S(1)} %copy-done.1, ...), custom_call_target="tpu_custom_call" | custom-call | tf_op jit(solution)/shard_map/pallas_call | solution.py:500
  103.7 0.7 copy.12
  104.4 0.7 copy.13
Async XLA Ops:
  0.6 0.7 copy-start.4
  1.3 0.7 copy-start.3
  2.0 0.9 copy-start
  2.9 0.9 copy-start.1
  3.9 0.9 copy-start.2

commit v3 on v0

v3 whole, which is shorter than its diff:
```python
import jax
import jax.numpy as jnp
from jax import lax
from jax.experimental import pallas as pl
from jax.experimental.pallas import tpu as pltpu
from jax.sharding import PartitionSpec as P

MESH = pl.DeviceIdType.MESH
F32 = jnp.float32
BF16 = jnp.bfloat16
VMEM = 60 << 20
HOME = ((8, 6, 10, 4, 12, 2, 14, 0), (7, 9, 5, 11, 3, 13, 1, 15))
HELD = 6
DIRECT = 6
FAR = ((8, 4, 12, 0, 6, 10, 2, 14), (7, 9, 1, 15, 5, 11, 3, 13))


def kernel(
    anc_v, pole_s, table_s, panel_h, inv_h, diag_h,
    off, dens,
    panel, inv, diag, left, wt, ar, pr, lr, buf, lbuf, ancb_v, ancb_s, wtb, prow, xb, yt, d, rx, fb, rz, wd, dg, res,
    reach_sem, in_sem, one_sem,
    p_send, p_recv, l_send, l_recv, h_send, h_recv, pz_send, pz_recv, lz_send, lz_recv, a_send, a_recv, w_send, w_recv,
    xg_send, xg_recv, yg_send, yg_recv, cg_send, cg_recv, cr_send, cr_recv,
    ly_send, ly_recv, lc_send, lc_recv,
    g_send, g_recv, r_send, o_recv, xr_send, xr_recv, z_send, z_recv, n_send, n_recv,
):
    g = lax.axis_index("grid")
    p = lax.axis_index("pole")
    z, xl = g // 2, g % 2
    y, xh, core = p // 4, (p // 2) % 2, p % 2
    u = 2 * y + core
    x = 2 * xh + xl
    half = z // 2
    odd = z % 2
    own_parity = 1 - lax.rem(xh + xl, 2)
    part = lax.rem(x + 3 + 2 * odd, 4)
    parity = part // 2
    pole_core = lax.rem(z + own_parity, 2)
    passed_part = 2 * odd + 1 - xl
    partner = p + 1 - 2 * core
    gx = g + 1 - 2 * xl

    def remote(src, dst, send, recv, pole, grid):
        return pltpu.make_async_remote_copy(
            src_ref=src, dst_ref=dst, send_sem=send, recv_sem=recv,
            device_id={"pole": pole, "grid": grid}, device_id_type=MESH,
        )

    def wait_in(ref, sem):
        remote(ref, ref, sem, sem, partner, g).wait_recv()

    def wait_out(ref, sem):
        remote(ref, ref, sem, sem, partner, g).wait_send()

    def other(pole, grid):
        return jnp.logical_or(pole != p, grid != g)

    def each(count, body):
        def step(n, carry):
            body(n)
            return carry

        lax.fori_loop(0, count, step, 0)

    def aligned(n, size):
        return pl.ds(pl.multiple_of(n * size, size), size)

    barrier = pltpu.get_barrier_semaphore()

    def hello(pole, grid):
        @pl.when(other(pole, grid))
        def _():
            pl.semaphore_signal(barrier, inc=1, device_id={"pole": pole, "grid": grid}, device_id_type=MESH)

    loads = [
        pltpu.make_async_copy(inv_h, inv, in_sem.at[0]),
        pltpu.make_async_copy(panel_h, panel, in_sem.at[1]),
        pltpu.make_async_copy(diag_h, diag, in_sem.at[2]),
    ]
    for load in loads:
        load.start()
    next_z, last_z = [2 * lax.rem(z + k, 16) + xl for k in (1, 15)]
    hello(p, next_z)
    hello(p, last_z)
    each(32, lambda n: hello(n // 2, 2 * z + n % 2))
    loads[0].wait()
    for k in range(0, 8, 2):
        left[:, 64 * k : 64 * k + 128] = jnp.concatenate(
            [inv[0, 0, k].reshape(128, 64), inv[0, 0, k + 1].reshape(128, 64)], axis=1
        )
    loads[1].wait()
    pl.semaphore_wait(barrier, 2 + 31)

    def reach(n):
        for k in (1 << n, 16 - (1 << n)):
            pl.semaphore_signal(
                reach_sem.at[n], inc=1,
                device_id={"pole": p, "grid": 2 * lax.rem(z + k, 16) + xl}, device_id_type=MESH,
            )

    reach(0)

    def target(n):
        return (n // 2) * 4 + lax.rem(xl + odd + core, 2) * 2 + n % 2

    def send_l(k):
        n = lax.rem(u + k, 8)
        piece = left.at[aligned(n % 2, 64), aligned(n // 2, 128)]
        remote(piece, lr.at[p // 2], l_send, l_recv.at[p // 2], target(n), gx).start()

    def send_p(k):
        n = lax.rem(u + k, 8)
        remote(panel.at[0, :, :, aligned(n, 128)], pr.at[p // 2], p_send, p_recv.at[p // 2], target(n), gx).start()

    @pl.when(xh == 0)
    def _():
        for n in range(2):
            remote(anc_v, ar, h_send.at[n], h_recv, target(2 * y + n), gx).start()

    each(8, send_l)
    each(8, send_p)
    for n in range(3):
        pl.semaphore_wait(reach_sem.at[n], 2)
        if n < 2:
            reach(n + 1)

    index = pole_s[0]
    my_wr = table_s[0, index]
    my_wi = table_s[1, index]
    is_real = lax.broadcasted_iota(jnp.int32, (8, 128), 0) == 0
    wt[...] = jnp.where(is_real, my_wr, my_wi)

    @pl.when(z == p)
    def _():
        def send_w(q):
            @pl.when(q != p)
            def _():
                remote(wt, wtb, w_send.at[q], w_recv, q, g).start()

        wtb[...] = wt[...]
        each(16, send_w)

    l_place = (aligned(core, 64), aligned(y, 128))

    def pole_of(n):
        from_u = lax.rem(u + 8 - 2 * (n // 2) - lax.rem(core + pole_core, 2), 8)
        return (from_u // 2) * 4 + (n % 2) * 2 + pole_core

    def pole_far(n):
        return lax.rem(z + jnp.where(own_parity == 0, FAR[0][n], FAR[1][n]), 16)

    def pass_l(n):
        q = pole_of(n)
        ref = lr.at[q // 2]
        wait_in(ref, l_recv.at[q // 2])

        @pl.when(q != z)
        def _():
            remote(ref, lbuf.at[(half,) + l_place], lz_send, lz_recv.at[half], p, 2 * q + xl).start()

    def pass_p(n):
        q = pole_far(n)
        ref = pr.at[q // 2]
        wait_in(ref, p_recv.at[q // 2])

        @pl.when(q != z)
        def _():
            remote(ref, buf.at[half, passed_part], pz_send.at[n // 4], pz_recv.at[half], p, 2 * q + xl).start()

    def pass_a(n):
        q = 2 * n + pole_core

        @pl.when(q != z)
        def _():
            remote(ar, ancb_v.at[half], a_send.at[n], a_recv.at[half], p, 2 * q + xl).start()

    def sent(ref, sem, count):
        @pl.when(own_parity == 0)
        def _():
            wait_out(ref.at[0 : count - 1], sem)

        @pl.when(own_parity != 0)
        def _():
            wait_out(ref.at[0:count], sem)

    each(8, pass_l)
    sent(lr, lz_send, 8)
    for n in range(4):
        pass_p(n)
    wait_in(ar, h_recv)
    each(8, pass_a)

    @pl.when(own_parity == 0)
    def _():
        copies = [
            pltpu.make_async_copy(lr.at[half], lbuf.at[(half,) + l_place], one_sem.at[1]),
            pltpu.make_async_copy(ar, ancb_v.at[half], one_sem.at[2]),
        ]
        for copy in copies:
            copy.start()
        for copy in copies:
            copy.wait()

    loads[2].wait()
    for n in range(8):
        wd[n] = my_wr * diag[0, :, 128 * n : 128 * n + 128] - my_wi * diag[0, :, 1024 + 128 * n : 1152 + 128 * n]

    def holder(n):
        return (n // 4) * 4 + xl * 2 + (n // 2) % 2, 2 * z + n % 2

    def send_d(n):
        pole, grid = holder(n)

        @pl.when(other(pole, grid))
        def _():
            remote(wd.at[n // 2, aligned(n % 2, 16)], dg.at[p], g_send, g_recv, pole, grid).start()

    each(16, send_d)

    @pl.when(xl == xh)
    def _():
        dg[p] = wd[u, aligned(xl, 16)]

    def at_x(k):
        to = lax.rem(x + k, 4)
        return y * 4 + (to // 2) * 2 + core, 2 * z + to % 2

    def at_y(k):
        return lax.rem(y + k, 4) * 4 + xh * 2 + core

    def from_z(m, ref, sem):
        @pl.when(2 * m + parity != z)
        def _():
            wait_in(ref, sem.at[m])

    for m in range(8):
        from_z(m, lbuf.at[(m,) + l_place], lz_recv)

    def l_of(k, rows):
        return lbuf.at[rows, aligned(core, 64), aligned(lax.rem(y + k, 4), 128)]

    whole = slice(0, 8)
    for k, n in ((1, 0), (3, 1)):
        ref = l_of(0, whole)
        remote(ref, ref, ly_send.at[0], ly_recv.at[n], at_y(k), g).start()
    sent(pr, pz_send.at[0], 4)
    for n in range(4, 8):
        pass_p(n)

    @pl.when(own_parity == 0)
    def _():
        copy = pltpu.make_async_copy(pr.at[half], buf.at[half, part], one_sem.at[0])
        copy.start()
        copy.wait()

    for k, n, to, rows in ((3, 0, 1, slice(0, 4)), (1, 1, 3, slice(4, 8))):
        wait_in(l_of(k, whole), ly_recv.at[n])
        ref = l_of(k, rows)
        remote(ref, ref, ly_send.at[1], ly_recv.at[2 + n], at_y(to), g).start()
    for m in range(8):
        from_z(m, ancb_v.at[m], a_recv)
    small = pltpu.make_async_copy(ancb_v, ancb_s, one_sem.at[0])
    small.start()

    def far_m(own, i):
        return lax.rem(z + 16 - jnp.where(own == 0, FAR[0][i], FAR[1][i]), 16) // 2

    def x_part(k):
        return lax.rem(part + k, 4)

    def x_own(k):
        to = lax.rem(x + k, 4)
        return 1 - lax.rem(to // 2 + to % 2, 2)

    def y_part(k):
        return 2 * lax.rem(y + k, 4) + core

    ways = ((1, 0), (3, 1))
    rows_here = lbuf.at[:, aligned(core, 64), :]

    def start_one(i):
        m = far_m(own_parity, i)
        block = buf.at[m, part]
        there = prow.at[u, m]
        for k, n in ways + (((2, 2),) if i >= DIRECT else ()):
            pole, grid = at_x(k)
            remote(block, block, xg_send, xg_recv.at[n, i], pole, grid).start()
            remote(block, there, yg_send, yg_recv.at[n, i], at_y(k), g).start()
        remote(block, there, cg_send, cg_recv, partner, g).start()
        prow[u, m] = buf[m, part]

    def pass_one(i):
        m = far_m(own_parity, i)
        for k, n in ((3, 0), (1, 1)):
            ref = buf.at[far_m(x_own(k), i), x_part(k)]
            wait_in(ref, xg_recv.at[n, i])
            if i < DIRECT and i % 2 == n:
                pole, grid = at_x(4 - k)
                remote(ref, ref, xg_send, xg_recv.at[2, i], pole, grid).start()
        for k, n in ((3, 0), (1, 1)):
            ref = prow.at[y_part(k), m]
            wait_in(ref, yg_recv.at[n, i])
            if i < DIRECT and i % 2 == n:
                remote(ref, ref, yg_send, yg_recv.at[2, i], at_y(4 - k), g).start()

    def arrived(i):
        from_z(far_m(own_parity, i), buf.at[far_m(own_parity, i), part], pz_recv)

    for i in range(4):
        arrived(i)
        start_one(i)
    for n, rows in ((0, slice(0, 4)), (1, slice(4, 8))):
        wait_in(l_of(2, rows), ly_recv.at[2 + n])
    remote(rows_here, rows_here, lc_send, lc_recv, partner, g).start()
    for i in range(4):
        pass_one(i)
    for i in range(4, 8):
        arrived(i)
        start_one(i)
    for i in range(4, 8):
        pass_one(i)

    def send_cr(k):
        came = prow.at[y_part(k)]
        remote(came, came, cr_send, cr_recv, partner, g).start()

    send_cr(3)
    send_cr(1)
    for i in range(8):
        wait_in(buf.at[far_m(x_own(2), i), x_part(2)], xg_recv.at[2, i])
    for i in range(8):
        wait_in(prow.at[y_part(2), far_m(own_parity, i)], yg_recv.at[2, i])
    send_cr(2)
    small.wait()
    wait_in(rows_here, lc_recv)

    @pl.when(z != p)
    def _():
        wait_in(wtb, w_recv)

    wr = wtb[0:1, :]
    wi = wtb[1:2, :]
    off_place = off.at[0, :, :, aligned(u, 128)]

    def send_home(i):
        m = lax.rem(z + 16 - jnp.where(own_parity == 0, HOME[0][i], HOME[1][i]), 16) // 2
        remote(xb.at[m], off_place, r_send, o_recv, z, 2 * (2 * m + parity) + 1 - xl).start()

    for m in range(8):
        rows = []
        for k in range(8):
            j = ancb_s[m, 0, k]
            rows.append(jnp.concatenate([buf[j // 4, j % 4, 0], buf[j // 4, j % 4, 1]], axis=1))
        both = jnp.dot(lbuf[m], jnp.concatenate(rows, axis=0), preferred_element_type=F32)
        real = both[64:, 128:] - both[:64, :128]
        imag = -(both[:64, 128:] + both[64:, :128])
        xb[m, 0] = real.astype(BF16)
        xb[m, 1] = imag.astype(BF16)
        term = jnp.concatenate([wr * real - wi * imag, -wr * imag - wi * real], axis=0).T
        high = term.astype(BF16)
        yt[0:128, 128 * m : 128 * m + 128] = high
        yt[128:256, 128 * m : 128 * m + 128] = (term - high.astype(F32)).astype(BF16)

    for i in range(HELD):
        send_home(i)
    wait_in(prow.at[0], cg_recv)
    wait_in(prow.at[0:3], cr_recv)
    for n in range(4):
        columns = jnp.concatenate([prow[2 * n].reshape(1024, 128), prow[2 * n + 1].reshape(1024, 128)], axis=1)
        two = jnp.dot(yt[...], columns, preferred_element_type=F32)
        one = two[:128] + two[128:]
        d[4 * n : 4 * n + 2] = one[:, :128].T.reshape(2, 64, 128)
        d[4 * n + 2 : 4 * n + 4] = one[:, 128:].T.reshape(2, 64, 128)

    for h in range(2):
        for k in (2, 1, 3):
            pole, grid = at_x(k)
            there = pl.ds(pl.multiple_of(lax.rem(x + k, 4) * 16 + 8 * h, 8), 8)
            remote(d.at[:, there], rx.at[h, k - 1], xr_send, xr_recv.at[h], pole, grid).start()

    for h in range(2):
        wait_in(rx.at[h], xr_recv.at[h])
        here = pl.ds(pl.multiple_of(x * 16 + 8 * h, 8), 8)
        fb[h] = d[:, here] + rx[h, 0] + rx[h, 1] + rx[h, 2]

        def send_z(n):
            to = lax.rem(z + jnp.where(n % 2 == 0, 8 + n // 2, 7 - n // 2), 16)
            remote(fb.at[h, to], rz.at[h, z], z_send.at[h], z_recv.at[h], p, 2 * to + xl).start()

        each(15, send_z)
    for i in range(HELD, 8):
        send_home(i)

    @pl.when(xl == xh)
    def _():
        wait_in(dg.at[0:15], g_recv)

    @pl.when(xl != xh)
    def _():
        wait_in(dg, g_recv)

    total = dg[0]
    for n in range(1, 16):
        total = total + dg[n]
    for h in range(2):
        rz[h, z] = fb[h, z]
        wait_in(rz.at[h, 0:15], z_recv.at[h])
        minus = rz[h, 0]
        for n in range(1, 16):
            minus = minus + rz[h, n]
        res[8 * h : 8 * h + 8] = total[8 * h : 8 * h + 8] - minus

    place = dens.at[aligned(xl, 16), aligned(u, 128)]

    def send_n(k):
        n = lax.rem(p + k, 16)

        @pl.when(other(n, 2 * z + xh))
        def _():
            remote(res, place, n_send, n_recv, n, 2 * z + xh).start()

    each(16, send_n)

    @pl.when(xl == xh)
    def _():
        copy = pltpu.make_async_copy(res, place, one_sem.at[2])
        copy.start()
        copy.wait()

    wait_out(left, l_send)
    wait_out(panel, p_send)

    @pl.when(xh == 0)
    def _():
        for n in range(2):
            wait_out(ar, h_send.at[n])

    @pl.when(z == p)
    def _():
        def done_w(q):
            @pl.when(q != p)
            def _():
                wait_out(wt, w_send.at[q])

        each(16, done_w)

    def done_a(n):
        @pl.when(2 * n + pole_core != z)
        def _():
            wait_out(ar, a_send.at[n])

    each(8, done_a)

    wait_out(pr.at[0:4], pz_send.at[1])
    wait_out(lbuf.at[:, 0:64, 0:256], ly_send.at[0])
    wait_out(lbuf.at[:, 0:64, 0:128], ly_send.at[1])
    wait_out(rows_here, lc_send)
    wait_out(prow.at[0:3], xg_send)
    wait_out(prow.at[0:3], yg_send)
    wait_out(prow.at[0], cg_send)
    wait_out(prow.at[0:3], cr_send)
    wait_out(xb, r_send)
    wait_out(rx, xr_send)
    for h in range(2):
        wait_out(fb.at[h, 0:15], z_send.at[h])

    @pl.when(xl == xh)
    def _():
        wait_out(dg.at[0:15], g_send)
        wait_out(dg.at[0:15], n_send)
        wait_in(dg.at[0:15], n_recv)

    @pl.when(xl != xh)
    def _():
        wait_out(dg, g_send)
        wait_out(dg, n_send)
        wait_in(dg, n_recv)

    wait_in(xb, o_recv)


def shards(panel, inverse_blocks, diag_inverse, ancestors, pole_index, weight_table):
    vmem = pl.BlockSpec(memory_space=pltpu.VMEM)
    smem = pl.BlockSpec(memory_space=pltpu.SMEM)
    hbm = pl.BlockSpec(memory_space=pl.ANY)
    dma = pltpu.SemaphoreType.DMA
    scratch = [
        pltpu.VMEM((1, 2, 64, 1024), BF16),
        pltpu.VMEM((1, 1, 8, 2, 64, 64), BF16),
        pltpu.VMEM((1, 32, 2048), F32),
        pltpu.VMEM((128, 512), BF16),
        pltpu.VMEM((8, 128), F32),
        pltpu.VMEM((1, 8), jnp.int32),
        pltpu.VMEM((8, 2, 64, 128), BF16),
        pltpu.VMEM((8, 64, 128), BF16),
        pltpu.VMEM((8, 4, 2, 64, 128), BF16),
        pltpu.VMEM((8, 128, 512), BF16),
        pltpu.VMEM((8, 1, 8), jnp.int32),
        pltpu.SMEM((8, 1, 8), jnp.int32),
        pltpu.VMEM((8, 128), F32),
        pltpu.VMEM((8, 8, 2, 64, 128), BF16),
        pltpu.VMEM((8, 2, 64, 128), BF16),
        pltpu.VMEM((256, 1024), BF16),
        pltpu.VMEM((16, 64, 128), F32),
        pltpu.VMEM((2, 3, 16, 8, 128), F32),
        pltpu.VMEM((2, 16, 8, 128), F32),
        pltpu.VMEM((2, 16, 8, 128), F32),
        pltpu.VMEM((8, 32, 128), F32),
        pltpu.VMEM((16, 16, 128), F32),
        pltpu.VMEM((16, 128), F32),
        pltpu.SemaphoreType.REGULAR((3,)), dma((3,)), dma((3,)),
        dma, dma((8,)), dma, dma((8,)), dma((2,)), dma, dma((2,)), dma((8,)), dma, dma((8,)), dma((8,)), dma((8,)), dma((16,)), dma,
        dma, dma((3, 8)), dma, dma((3, 8)), dma, dma, dma, dma,
        dma((2,)), dma((4,)), dma, dma,
        dma, dma, dma, dma, dma, dma((2,)), dma((2,)), dma((2,)), dma, dma,
    ]
    return pl.pallas_call(
        kernel,
        out_shape=(
            jax.ShapeDtypeStruct(panel.shape, BF16),
            jax.ShapeDtypeStruct((32, 1024), F32),
        ),
        in_specs=[vmem, smem, smem, hbm, hbm, hbm],
        out_specs=(hbm, hbm),
        scratch_shapes=scratch,
        compiler_params=pltpu.CompilerParams(
            collective_id=1, has_side_effects=True, vmem_limit_bytes=VMEM
        ),
    )(ancestors, pole_index, weight_table.T, panel, inverse_blocks, diag_inverse)


def solution(mesh):
    placed = (
        P("pole", None, "grid", None),
        P("pole", "grid", None, None, None, None),
        P("pole", "grid", None),
        P("grid", None),
        P("pole"),
        P(),
    )
    return jax.shard_map(
        shards,
        mesh=mesh,
        in_specs=placed,
        out_specs=(P("pole", None, "grid", None), P("grid", None)),
        check_vma=False,
    )
```

time: 538 us -> 84.8 us (0.16)
  waiting for transfers between devices: 495 us -> 0 us
  Pallas kernels: 0 us -> 81 us
  between operations: 14.5 us -> 1.29 us
  matrix products: 10.2 us -> 0 us
  local copies, waits for them, and re-layouts: 11.3 us -> 2.36 us
  other arithmetic: 6.64 us -> 0 us
    all_gather x1 -> x0, waiting for transfers between devices: 198 us -> none  [shards(): piece = lax.all_gather(panel, 'grid', axis=2, tiled=True)]
    psum x1 -> x0, waiting for transfers between devices: 174 us -> none  [shards(): density = lax.psum(weighted, 'pole')]
    unnamed x4 -> x0, waiting for transfers between devices: 123 us -> none
    pallas_call x0 -> x1, Pallas kernels: none -> 81 us  [shards(): pl.pallas_call(kernel, out_shape=(jax.ShapeDtypeStruct(panel.shape, BF16)...]
    dot_general x3 -> x0, matrix products: 10.2 us -> none  [the longest x1 5.47 us: shards(): product = jnp.dot(left, right, preferred_element_type=jnp.float32)]
    unnamed x12 -> x4, local copies, waits for them, and re-layouts: 9.68 us -> 2.36 us
    sub x2 -> x0, other arithmetic: 6.4 us -> none  [the longest x1 4.25 us: shards(): weights[0] * both[:, :width] - weights[1] * both[:, width:]]
  transfers between devices with their start and end apart: 3 -> 0, of which waited for: 3 -> 0; matrix products, arithmetic and copies ran while one was open for 1% -> 0% of each run, Pallas kernels for 0% -> 0%
where the time goes in v3:
time: 84.8 us; the launch traced here: 84.6 us
  Pallas kernels  81 us (96%)
  local copies, waits for them, and re-layouts  2.36 us (3%)
  between operations  1.29 us (2%)
    pallas_call x1, Pallas kernels, shards(): pl.pallas_call(kernel, out_shape=(jax.ShapeDtypeStruct(panel.shape, BF16)...  81 us
    unnamed x4, local copies, waits for them, and re-layouts  2.36 us

profile of v3, /device:TPU:1, one launch (start us, length us, event | category | flops | bytes accessed | tf_op | source)
XLA Modules:
  0.0 84.6 jit_solution(5199763071083516568)
XLA Ops:
  1.3 81.0 %shard_map.77 = (bf16[1,2,64,1024]{3,2,1,0:T(8,128)(2,1)}, f32[32,1024]{1,0:T(8,128)}) custom-call(s32[1,8]{1,0:T(1,128)} %anc_v.1, s32[1]{0:T(128)S(6)} %copy.10.pole_s, f32[2,64]{1,0:T(2,128)} %bitcast.1, bf16[1,2,64,1024]{3,2,1,0:T(8,128)(2,1)} %panel_h.1, bf16[1,1,8,2,64,64]{5,4,3,2,1,0:T(8,128)(2,1)} %inv_h.1, f32[1,32,2048]{2,1,0:T(8,128)} %diag_h.1), custom_call_target="tpu_custom_call" | custom-call | tf_op jit(solution)/shard_map/pallas_call | solution.py:518
  82.3 0.0 copy-start
  82.3 1.7 %copy.11 = bf16[1,2,64,1024]{3,2,1,0:T(8,128)(2,1)} copy(bf16[1,2,64,1024]{3,2,1,0:T(8,128)(2,1)} %get-tuple-element.4) | data formatting | bytes 524288
  84.0 0.0 copy-done
  84.0 0.7 copy.12
Async XLA Ops:
  82.3 1.7 %copy-start = (f32[32,1024]{1,0:T(8,128)S(1)}, f32[32,1024]{1,0:T(8,128)}, u32[]{:S(2)}) copy-start(f32[32,1024]{1,0:T(8,128)} %get-tuple-element.5) | copy-start | bytes 393220

commit v4 on v3

--- a/solution.py
+++ b/solution.py
@@ -10,8 +10,8 @@
 BF16 = jnp.bfloat16
 VMEM = 60 << 20
 HOME = ((8, 6, 10, 4, 12, 2, 14, 0), (7, 9, 5, 11, 3, 13, 1, 15))
-HELD = 6
-DIRECT = 6
+HELD = 5
+DIRECT = 5
 FAR = ((8, 4, 12, 0, 6, 10, 2, 14), (7, 9, 1, 15, 5, 11, 3, 13))
 
 
@@ -313,9 +313,8 @@
     for n, rows in ((0, slice(0, 4)), (1, slice(4, 8))):
         wait_in(l_of(2, rows), ly_recv.at[2 + n])
     remote(rows_here, rows_here, lc_send, lc_recv, partner, g).start()
-    for i in range(4):
-        pass_one(i)
     for i in range(4, 8):
+        pass_one(i - 4)
         arrived(i)
         start_one(i)
     for i in range(4, 8):
@@ -395,10 +394,46 @@
     @pl.when(xl == xh)
     def _():
         wait_in(dg.at[0:15], g_recv)
+        wait_out(dg.at[0:15], g_send)
 
     @pl.when(xl != xh)
     def _():
         wait_in(dg, g_recv)
+        wait_out(dg, g_send)
+
+    wait_out(left, l_send)
+    wait_out(panel, p_send)
+
+    @pl.when(xh == 0)
+    def _():
+        for n in range(2):
+            wait_out(ar, h_send.at[n])
+
+    @pl.when(z == p)
+    def _():
+        def done_w(q):
+            @pl.when(q != p)
+            def _():
+                wait_out(wt, w_send.at[q])
+
+        each(16, done_w)
+
+    def done_a(n):
+        @pl.when(2 * n + pole_core != z)
+        def _():
+            wait_out(ar, a_send.at[n])
+
+    each(8, done_a)
+
+    wait_out(pr.at[0:4], pz_send.at[1])
+    wait_out(lbuf.at[:, 0:64, 0:256], ly_send.at[0])
+    wait_out(lbuf.at[:, 0:64, 0:128], ly_send.at[1])
+    wait_out(rows_here, lc_send)
+    wait_out(prow.at[0:3], xg_send)
+    wait_out(prow.at[0:3], yg_send)
+    wait_out(prow.at[0], cg_send)
+    wait_out(prow.at[0:3], cr_send)
+    wait_out(rx, xr_send)
 
     total = dg[0]
     for n in range(1, 16):
@@ -428,52 +463,17 @@
         copy.start()
         copy.wait()
 
-    wait_out(left, l_send)
-    wait_out(panel, p_send)
-
-    @pl.when(xh == 0)
-    def _():
-        for n in range(2):
-            wait_out(ar, h_send.at[n])
-
-    @pl.when(z == p)
-    def _():
-        def done_w(q):
-            @pl.when(q != p)
-            def _():
-                wait_out(wt, w_send.at[q])
-
-        each(16, done_w)
-
-    def done_a(n):
-        @pl.when(2 * n + pole_core != z)
-        def _():
-            wait_out(ar, a_send.at[n])
-
-    each(8, done_a)
-
-    wait_out(pr.at[0:4], pz_send.at[1])
-    wait_out(lbuf.at[:, 0:64, 0:256], ly_send.at[0])
-    wait_out(lbuf.at[:, 0:64, 0:128], ly_send.at[1])
-    wait_out(rows_here, lc_send)
-    wait_out(prow.at[0:3], xg_send)
-    wait_out(prow.at[0:3], yg_send)
-    wait_out(prow.at[0], cg_send)
-    wait_out(prow.at[0:3], cr_send)
     wait_out(xb, r_send)
-    wait_out(rx, xr_send)
     for h in range(2):
         wait_out(fb.at[h, 0:15], z_send.at[h])
 
     @pl.when(xl == xh)
     def _():
-        wait_out(dg.at[0:15], g_send)
         wait_out(dg.at[0:15], n_send)
         wait_in(dg.at[0:15], n_recv)
 
     @pl.when(xl != xh)
     def _():
-        wait_out(dg, g_send)
         wait_out(dg, n_send)
         wait_in(dg, n_recv)
 

time: 84.8 us -> 82.3 us (0.971)
  Pallas kernels: 81 us -> 78.4 us
    pallas_call x1, Pallas kernels: 81 us -> 78.4 us  [shards(): pl.pallas_call(kernel, out_shape=(jax.ShapeDtypeStruct(panel.shape, BF16)...]
where the time goes in v4:
time: 82.3 us; the launch traced here: 82.1 us
  Pallas kernels  78.4 us (95%)
  local copies, waits for them, and re-layouts  2.36 us (3%)
  between operations  1.29 us (2%)
    pallas_call x1, Pallas kernels, shards(): pl.pallas_call(kernel, out_shape=(jax.ShapeDtypeStruct(panel.shape, BF16)...  78.4 us
    unnamed x4, local copies, waits for them, and re-layouts  2.36 us

profile of v4, /device:TPU:1, one launch (start us, length us, event | category | flops | bytes accessed | tf_op | source)
XLA Modules:
  0.0 82.1 jit_solution(7122330172689130398)
XLA Ops:
  1.3 78.4 %shard_map.77 = (bf16[1,2,64,1024]{3,2,1,0:T(8,128)(2,1)}, f32[32,1024]{1,0:T(8,128)}) custom-call(s32[1,8]{1,0:T(1,128)} %anc_v.1, s32[1]{0:T(128)S(6)} %copy.10.pole_s, f32[2,64]{1,0:T(2,128)} %bitcast.1, bf16[1,2,64,1024]{3,2,1,0:T(8,128)(2,1)} %panel_h.1, bf16[1,1,8,2,64,64]{5,4,3,2,1,0:T(8,128)(2,1)} %inv_h.1, f32[1,32,2048]{2,1,0:T(8,128)} %diag_h.1), custom_call_target="tpu_custom_call" | custom-call | tf_op jit(solution)/shard_map/pallas_call | solution.py:518
  79.7 0.0 copy-start
  79.7 1.7 %copy.11 = bf16[1,2,64,1024]{3,2,1,0:T(8,128)(2,1)} copy(bf16[1,2,64,1024]{3,2,1,0:T(8,128)(2,1)} %get-tuple-element.4) | data formatting | bytes 524288
  81.4 0.0 copy-done
  81.4 0.7 copy.12
Async XLA Ops:
  79.7 1.7 %copy-start = (f32[32,1024]{1,0:T(8,128)S(1)}, f32[32,1024]{1,0:T(8,128)}, u32[]{:S(2)}) copy-start(f32[32,1024]{1,0:T(8,128)} %get-tuple-element.5) | copy-start | bytes 393220

commit v5 on v4

--- a/solution.py
+++ b/solution.py
@@ -12,7 +12,7 @@
 HOME = ((8, 6, 10, 4, 12, 2, 14, 0), (7, 9, 5, 11, 3, 13, 1, 15))
 HELD = 5
 DIRECT = 5
-FAR = ((8, 4, 12, 0, 6, 10, 2, 14), (7, 9, 1, 15, 5, 11, 3, 13))
+FAR = ((0, 4, 12, 8, 6, 10, 2, 14), (1, 15, 7, 9, 5, 11, 3, 13))
 
 
 def kernel(
@@ -166,7 +166,7 @@
 
         @pl.when(q != z)
         def _():
-            remote(ref, buf.at[half, passed_part], pz_send.at[n // 4], pz_recv.at[half], p, 2 * q + xl).start()
+            remote(ref, buf.at[half, passed_part], pz_send.at[(0, 0, 1, 1, 2, 2, 2, 2)[n]], pz_recv.at[half], p, 2 * q + xl).start()
 
     def pass_a(n):
         q = 2 * n + pole_core
@@ -244,7 +244,7 @@
     for k, n in ((1, 0), (3, 1)):
         ref = l_of(0, whole)
         remote(ref, ref, ly_send.at[0], ly_recv.at[n], at_y(k), g).start()
-    sent(pr, pz_send.at[0], 4)
+    sent(pr, pz_send.at[0], 2)
     for n in range(4, 8):
         pass_p(n)
 
@@ -425,7 +425,8 @@
 
     each(8, done_a)
 
-    wait_out(pr.at[0:4], pz_send.at[1])
+    wait_out(pr.at[0:2], pz_send.at[1])
+    wait_out(pr.at[0:4], pz_send.at[2])
     wait_out(lbuf.at[:, 0:64, 0:256], ly_send.at[0])
     wait_out(lbuf.at[:, 0:64, 0:128], ly_send.at[1])
     wait_out(rows_here, lc_send)
@@ -510,7 +511,7 @@
         pltpu.VMEM((16, 16, 128), F32),
         pltpu.VMEM((16, 128), F32),
         pltpu.SemaphoreType.REGULAR((3,)), dma((3,)), dma((3,)),
-        dma, dma((8,)), dma, dma((8,)), dma((2,)), dma, dma((2,)), dma((8,)), dma, dma((8,)), dma((8,)), dma((8,)), dma((16,)), dma,
+        dma, dma((8,)), dma, dma((8,)), dma((2,)), dma, dma((3,)), dma((8,)), dma, dma((8,)), dma((8,)), dma((8,)), dma((16,)), dma,
         dma, dma((3, 8)), dma, dma((3, 8)), dma, dma, dma, dma,
         dma((2,)), dma((4,)), dma, dma,
         dma, dma, dma, dma, dma, dma((2,)), dma((2,)), dma((2,)), dma, dma,

time: 82.3 us -> 81.6 us (level)
  no operation moved by 1% of the time
where the time goes in v5:
time: 81.6 us; the launch traced here: 81.4 us
  Pallas kernels  77.8 us (95%)
  local copies, waits for them, and re-layouts  2.36 us (3%)
  between operations  1.29 us (2%)
    pallas_call x1, Pallas kernels, shards(): pl.pallas_call(kernel, out_shape=(jax.ShapeDtypeStruct(panel.shape, BF16)...  77.8 us
    unnamed x4, local copies, waits for them, and re-layouts  2.36 us

profile of v5, /device:TPU:1, one launch (start us, length us, event | category | flops | bytes accessed | tf_op | source)
XLA Modules:
  0.0 81.4 jit_solution(6492320809053745388)
XLA Ops:
  1.3 77.8 %shard_map.77 = (bf16[1,2,64,1024]{3,2,1,0:T(8,128)(2,1)}, f32[32,1024]{1,0:T(8,128)}) custom-call(s32[1,8]{1,0:T(1,128)} %anc_v.1, s32[1]{0:T(128)S(6)} %copy.10.pole_s, f32[2,64]{1,0:T(2,128)} %bitcast.1, bf16[1,2,64,1024]{3,2,1,0:T(8,128)(2,1)} %panel_h.1, bf16[1,1,8,2,64,64]{5,4,3,2,1,0:T(8,128)(2,1)} %inv_h.1, f32[1,32,2048]{2,1,0:T(8,128)} %diag_h.1), custom_call_target="tpu_custom_call" | custom-call | tf_op jit(solution)/shard_map/pallas_call | solution.py:519
  79.0 0.0 copy-start
  79.1 1.7 %copy.11 = bf16[1,2,64,1024]{3,2,1,0:T(8,128)(2,1)} copy(bf16[1,2,64,1024]{3,2,1,0:T(8,128)(2,1)} %get-tuple-element.4) | data formatting | bytes 524288
  80.8 0.0 copy-done
  80.8 0.7 copy.12
Async XLA Ops:
  79.0 1.7 %copy-start = (f32[32,1024]{1,0:T(8,128)S(1)}, f32[32,1024]{1,0:T(8,128)}, u32[]{:S(2)}) copy-start(f32[32,1024]{1,0:T(8,128)} %get-tuple-element.5) | copy-start | bytes 393220

commit v6 on v5

--- a/solution.py
+++ b/solution.py
@@ -479,6 +479,19 @@
         wait_in(dg, n_recv)
 
     wait_in(xb, o_recv)
+
+
+def hand_over(off_h, dens_h, off, dens, off_v, dens_v, sem):
+    ways = [(off_h, off_v, off), (dens_h, dens_v, dens)]
+    first = [pltpu.make_async_copy(a, b, sem.at[0, n]) for n, (a, b, _) in enumerate(ways)]
+    second = [pltpu.make_async_copy(b, c, sem.at[1, n]) for n, (_, b, c) in enumerate(ways)]
+    for copy in first:
+        copy.start()
+    for a, b in zip(first, second):
+        a.wait()
+        b.start()
+    for copy in second:
+        copy.wait()
 
 
 def shards(panel, inverse_blocks, diag_inverse, ancestors, pole_index, weight_table):
@@ -516,7 +529,7 @@
         dma((2,)), dma((4,)), dma, dma,
         dma, dma, dma, dma, dma, dma((2,)), dma((2,)), dma((2,)), dma, dma,
     ]
-    return pl.pallas_call(
+    results = pl.pallas_call(
         kernel,
         out_shape=(
             jax.ShapeDtypeStruct(panel.shape, BF16),
@@ -529,6 +542,17 @@
             collective_id=1, has_side_effects=True, vmem_limit_bytes=VMEM
         ),
     )(ancestors, pole_index, weight_table.T, panel, inverse_blocks, diag_inverse)
+    return pl.pallas_call(
+        hand_over,
+        out_shape=(
+            jax.ShapeDtypeStruct(panel.shape, BF16),
+            jax.ShapeDtypeStruct((32, 1024), F32),
+        ),
+        in_specs=[hbm, hbm],
+        out_specs=(hbm, hbm),
+        scratch_shapes=[pltpu.VMEM(panel.shape, BF16), pltpu.VMEM((32, 1024), F32), dma((2, 2))],
+        compiler_params=pltpu.CompilerParams(vmem_limit_bytes=VMEM),
+    )(*results)
 
 
 def solution(mesh):

time: 81.6 us -> 81 us (level)
  local copies, waits for them, and re-layouts: 2.36 us -> 0 us
  Pallas kernels: 77.8 us -> 79.5 us
    unnamed x4 -> x0, local copies, waits for them, and re-layouts: 2.36 us -> none
    pallas_call x0 -> x1, Pallas kernels: none -> 1.73 us  [shards(): pl.pallas_call(hand_over, out_shape=(jax.ShapeDtypeStruct(panel.shape, BF...]
where the time goes in v6:
time: 81 us; the launch traced here: 80.8 us
  Pallas kernels  79.5 us (98%)
  between operations  1.29 us (2%)
    pallas_call x1, Pallas kernels, shards(): pl.pallas_call(kernel, out_shape=(jax.ShapeDtypeStruct(panel.shape, BF16)...  77.8 us
    pallas_call x1, Pallas kernels, shards(): pl.pallas_call(hand_over, out_shape=(jax.ShapeDtypeStruct(panel.shape, BF...  1.73 us

profile of v6, /device:TPU:1, one launch (start us, length us, event | category | flops | bytes accessed | tf_op | source)
XLA Modules:
  0.0 80.8 jit_solution(11119467677549344608)
XLA Ops:
  1.3 77.8 %shard_map.77 = (bf16[1,2,64,1024]{3,2,1,0:T(8,128)(2,1)}, f32[32,1024]{1,0:T(8,128)}) custom-call(s32[1,8]{1,0:T(1,128)} %anc_v.1, s32[1]{0:T(128)S(6)} %copy.8.pole_s, f32[2,64]{1,0:T(2,128)} %bitcast.1, bf16[1,2,64,1024]{3,2,1,0:T(8,128)(2,1)} %panel_h.1, bf16[1,1,8,2,64,64]{5,4,3,2,1,0:T(8,128)(2,1)} %inv_h.1, f32[1,32,2048]{2,1,0:T(8,128)} %diag_h.1), custom_call_target="tpu_custom_call" | custom-call | tf_op jit(solution)/shard_map/pallas_call | solution.py:532
  79.1 1.7 %shard_map.78 = (bf16[1,2,64,1024]{3,2,1,0:T(8,128)(2,1)}, f32[32,1024]{1,0:T(8,128)}) custom-call(bf16[1,2,64,1024]{3,2,1,0:T(8,128)(2,1)} %get-tuple-element.4.off_h, f32[32,1024]{1,0:T(8,128)} %get-tuple-element.5.dens_h), custom_call_target="tpu_custom_call" | custom-call | tf_op jit(solution)/shard_map/pallas_call | solution.py:545
